TPU v7x, 32 devices: a whole 2x2x4 slice. The times are simulated.
32 devices in a mesh: sec: 4 (over x, core), col: 8 (over z, y).
Axes of the slice: x: 2, y: 2, z: 4, core: 2. Of those that a mesh axis runs over, the one named last changes fastest.
Arguments:
- rhs: bfloat16 [256, 64, 256], P(('sec', 'col')), may hold values from -6 to 6
- diag_inv: bfloat16 [256, 64, 64], P(('sec', 'col')), may hold values from -0.5 to 0.5
- off_tiles: bfloat16 [256, 16, 64, 64], P(('sec', 'col')), may hold values from -0.1875 to 0.1875
- targets: int32 [256, 16], P(('sec', 'col')), may hold values from 0 to 63, all different within a row
- row_slot: int32 [4, 64], P('sec'), may hold values from 0 to 63, each once within a row
Outputs:
- solution: bfloat16 [256, 64, 256], P(('sec', 'col'))
- handed_on: bfloat16 [256, 64, 256], P(('sec', 'col'))
Inputs may be any that keep to these rules, and one draw needn't show every extreme that they name: The 16 targets of one block are distinct. `row_slot`: each row is a permutation.
All inputs are finite; a program needn't handle non-finite values.
Results may differ from a plain program's by a relative error of at most 0.03.
Values may be sent and summed in bfloat16 or wider, within the bound.
A program may use at most 64 MiB of HBM per device.

v0:
```python
import jax
import jax.numpy as jnp
from jax import lax
from jax.sharding import PartitionSpec as P


def shifted(value, axis, by):
    length = lax.axis_size(axis)
    pairs = [(i, i + by) for i in range(length) if 0 <= i + by < length]
    return lax.ppermute(value, axis, pairs)


def solve_part(rhs_part, incoming, diag_inv, off_tiles, onehot):
    residual = (rhs_part.astype(jnp.float32) - incoming.astype(jnp.float32)).astype(jnp.bfloat16)
    solved = jnp.einsum(
        "kab,kbn->kan", diag_inv, residual, preferred_element_type=jnp.float32
    ).astype(jnp.bfloat16)
    tiles = jnp.einsum(
        "kpab,kbn->kpan", off_tiles, solved, preferred_element_type=jnp.float32
    ).astype(jnp.bfloat16)
    flat_tiles = tiles.reshape(tiles.shape[0] * tiles.shape[1], -1)
    partial_value = jnp.dot(onehot, flat_tiles, preferred_element_type=jnp.float32)
    return (solved, partial_value.reshape(onehot.shape[0], solved.shape[1], solved.shape[2]))


def advance(partial_value, sending):
    owned = lax.psum_scatter(
        partial_value.astype(jnp.bfloat16), "col", scatter_dimension=0, tiled=True
    )
    if sending:
        passed = shifted(owned, "sec", 1)
    else:
        passed = owned
    return (owned, passed)


def shards(rhs, diag_inv, off_tiles, targets, row_slot):
    blocks = rhs.shape[0]
    width = rhs.shape[1]
    columns = rhs.shape[2]
    segments = lax.axis_size("sec")
    rows_all = blocks * lax.axis_size("col")
    segment_id = lax.axis_index("sec")
    dest_slot = row_slot[0][targets].reshape(-1)
    onehot = (dest_slot[None, :] == jnp.arange(rows_all, dtype=jnp.int32)[:, None]).astype(
        jnp.bfloat16
    )
    solution = jnp.zeros((blocks, width, columns), jnp.bfloat16)
    handed_on = jnp.zeros((blocks, width, columns), jnp.bfloat16)
    incoming = jnp.zeros((blocks, width, columns), jnp.bfloat16)
    for moment in range(segments):
        solved, partial_value = solve_part(rhs, incoming, diag_inv, off_tiles, onehot)
        owned, incoming = advance(partial_value, moment + 1 < segments)
        active = segment_id == moment
        solution = jnp.where(active, solved, solution)
        handed_on = jnp.where(active, owned, handed_on)
    return (solution, handed_on)


def solution(mesh):
    return jax.shard_map(
        shards,
        mesh=mesh,
        in_specs=(
            P(("sec", "col"), None, None),
            P(("sec", "col"), None, None),
            P(("sec", "col"), None, None, None),
            P(("sec", "col"), None),
            P("sec", None),
        ),
        out_specs=(P(("sec", "col"), None, None), P(("sec", "col"), None, None)),
        check_vma=False,
    )
```

profile of v0, /device:TPU:7, one launch (start us, length us, event | category | flops | bytes accessed | tf_op | source)
XLA Modules:
  0.0 387.6 jit_solution(18238630507391707031)
XLA Ops:
  7.2 0.0 copy-start
  7.2 0.0 reduce-scatter.5.cloned.1.call-start
  7.2 0.8 compare_select_fusion
  8.1 0.1 reshape.31
  8.1 1.2 convolution_convert_fusion.7
  9.4 1.2 convolution_convert_fusion.3
  10.6 4.9 %copy.27 = bf16[16,8,64,256]{3,1,2,0:T(8,128)(2,1)} copy(bf16[16,8,64,256]{3,2,1,0:T(8,128)(2,1)S(1)} %bitcast.88) | data formatting | bytes 8388608
  15.5 6.4 %copy.15 = bf16[16384,128]{1,0:T(8,128)(2,1)} copy(bf16[16384,128]{0,1:T(8,128)(2,1)} %bitcast.81) | data formatting | bytes 8388608 | tf_op jit(solution)/shard_map/dot_general | solution.py:22
  21.9 1.2 gather_fusion
  23.1 3.7 fusion.19
  26.9 0.0 copy-start.2
  26.9 2.5 copy.38
  29.4 0.0 reduce-scatter.5.cloned.1.call-update
  29.5 0.0 reduce-scatter.7.cloned.1.call-start
  29.5 67.5 %reduce-scatter.5.cloned.1.call-done = bf16[8,64,256]{2,1,0:T(8,128)(2,1)} async-done(((bf16[64,64,256]{2,1,0:T(8,128)(2,1)}), bf16[8,64,256]{2,1,0:T(8,128)(2,1)}) %reduce-scatter.5.cloned.1.call-update) | async-done | bytes 262160 | tf_op jit(solution)/shard_map/reduce_scatter | solution.py:27
  97.0 1.5 collective-permute-start
  98.4 3.2 collective-permute-done
  101.7 0.2 convolution_convert_fusion.6
  101.9 1.2 convolution_convert_fusion.2
  103.1 4.9 %copy.28 = bf16[16,8,64,256]{3,1,2,0:T(8,128)(2,1)} copy(bf16[16,8,64,256]{3,2,1,0:T(8,128)(2,1)S(1)} %bitcast.89) | data formatting | bytes 8388608
  108.0 6.4 %copy.17 = bf16[16384,128]{1,0:T(8,128)(2,1)} copy(bf16[16384,128]{0,1:T(8,128)(2,1)} %bitcast.82) | data formatting | bytes 8388608 | tf_op jit(solution)/shard_map/dot_general | solution.py:22
  114.4 3.7 fusion.17
  118.1 2.5 copy.37
  120.6 0.0 reduce-scatter.7.cloned.1.call-update
  120.7 0.0 reduce-scatter.9.cloned.1.call-start
  120.7 70.1 %reduce-scatter.7.cloned.1.call-done = bf16[8,64,256]{2,1,0:T(8,128)(2,1)} async-done(((bf16[64,64,256]{2,1,0:T(8,128)(2,1)}), bf16[8,64,256]{2,1,0:T(8,128)(2,1)}) %reduce-scatter.7.cloned.1.call-update) | async-done | bytes 262160 | tf_op jit(solution)/shard_map/reduce_scatter | solution.py:27
  190.8 1.5 collective-permute-start.1
  192.3 3.2 collective-permute-done.1
  195.5 0.2 convolution_convert_fusion.5
  195.7 1.2 convolution_convert_fusion.1
  197.0 4.9 %copy.29 = bf16[16,8,64,256]{3,1,2,0:T(8,128)(2,1)} copy(bf16[16,8,64,256]{3,2,1,0:T(8,128)(2,1)S(1)} %bitcast.90) | data formatting | bytes 8388608
  201.8 6.4 %copy.19 = bf16[16384,128]{1,0:T(8,128)(2,1)} copy(bf16[16384,128]{0,1:T(8,128)(2,1)} %bitcast.84) | data formatting | bytes 8388608 | tf_op jit(solution)/shard_map/dot_general | solution.py:22
  208.2 3.7 fusion.15
  212.0 2.5 copy.36
  214.5 0.0 reduce-scatter.9.cloned.1.call-update
  214.5 0.0 reduce-scatter.11.cloned.1.call-start
  214.6 70.2 %reduce-scatter.9.cloned.1.call-done = bf16[8,64,256]{2,1,0:T(8,128)(2,1)} async-done(((bf16[64,64,256]{2,1,0:T(8,128)(2,1)}), bf16[8,64,256]{2,1,0:T(8,128)(2,1)}) %reduce-scatter.9.cloned.1.call-update) | async-done | bytes 262160 | tf_op jit(solution)/shard_map/reduce_scatter | solution.py:27
  284.7 1.5 collective-permute-start.2
  286.3 3.1 collective-permute-done.2
  289.4 0.9 fusion.11
  290.4 1.2 convolution_convert_fusion
  291.6 4.9 %copy.30 = bf16[16,8,64,256]{3,1,2,0:T(8,128)(2,1)} copy(bf16[16,8,64,256]{3,2,1,0:T(8,128)(2,1)S(1)} %bitcast.86) | data formatting | bytes 8388608
  296.5 6.4 %copy.21 = bf16[16384,128]{1,0:T(8,128)(2,1)} copy(bf16[16384,128]{0,1:T(8,128)(2,1)} %bitcast.87) | data formatting | bytes 8388608 | tf_op jit(solution)/shard_map/dot_general | solution.py:22
  302.9 3.7 fusion.13
  306.7 2.5 copy.35
  309.2 0.0 reduce-scatter.11.cloned.1.call-update
  309.2 70.2 %reduce-scatter.11.cloned.1.call-done = bf16[8,64,256]{2,1,0:T(8,128)(2,1)} async-done(((bf16[64,64,256]{2,1,0:T(8,128)(2,1)}), bf16[8,64,256]{2,1,0:T(8,128)(2,1)}) %reduce-scatter.11.cloned.1.call-update) | async-done | bytes 262160 | tf_op jit(solution)/shard_map/reduce_scatter | solution.py:27
  379.4 1.7 select_select_fusion
  (13 shorter events, 0.0 us)
Async XLA Ops:
  7.2 2.2 copy-start
  7.2 89.8 %reduce-scatter.5.cloned.1.call-start = ((), (), s32[]{:S(2)}) async-start(), calls=%async_computation.4 | async-start | bytes 2359296 | tf_op jit(solution)/shard_map/reduce_scatter | solution.py:27
  15.5 6.4 %copy-start.1 = (s32[1,64]{1,0:T(1,128)S(1)}, s32[1,64]{1,0:T(1,128)}, u32[]{:S(2)}) copy-start(s32[1,64]{1,0:T(1,128)} %param.9) | copy-start | bytes 772
  26.9 74.8 %copy-start.2 = (bf16[8,64,256]{2,1,0:T(8,128)(2,1)S(1)}, bf16[8,64,256]{2,1,0:T(8,128)(2,1)}, u32[]{:S(2)}) copy-start(bf16[8,64,256]{2,1,0:T(8,128)(2,1)} %param.5) | copy-start | bytes 786436
  26.9 74.7 %copy-start.3 = (bf16[8,64,64]{2,1,0:T(8,128)(2,1)S(1)}, bf16[8,64,64]{2,1,0:T(8,128)(2,1)}, u32[]{:S(2)}) copy-start(bf16[8,64,64]{2,1,0:T(8,128)(2,1)} %param.6) | copy-start | bytes 196612
  29.5 161.3 %reduce-scatter.7.cloned.1.call-start = ((), (), s32[]{:S(2)}) async-start(), calls=%async_computation.5 | async-start | bytes 2359296 | tf_op jit(solution)/shard_map/reduce_scatter | solution.py:27
  97.0 4.7 %collective-permute-start = (bf16[8,64,256]{2,1,0:T(8,128)(2,1)}, bf16[8,64,256]{2,1,0:T(8,128)(2,1)S(1)}, u32[]{:S(2)}, u32[]{:S(2)}) collective-permute-start(bf16[8,64,256]{2,1,0:T(8,128)(2,1)} %reduce-scatter.5.cloned.1.call-done), channel_id=1, source_target_pairs={{0,8},{8,16},{16,24},{1,9},{9,17},{17,25},{2,10},{10,18},{18,26},{... | collective-permute-start | bytes 786440 | tf_op jit(solution)/shard_map/ppermute | solution.py:10
  120.7 164.1 %reduce-scatter.9.cloned.1.call-start = ((), (), s32[]{:S(2)}) async-start(), calls=%async_computation.6 | async-start | bytes 2359296 | tf_op jit(solution)/shard_map/reduce_scatter | solution.py:27
  190.8 4.7 %collective-permute-start.1 = (bf16[8,64,256]{2,1,0:T(8,128)(2,1)}, bf16[8,64,256]{2,1,0:T(8,128)(2,1)S(1)}, u32[]{:S(2)}, u32[]{:S(2)}) collective-permute-start(bf16[8,64,256]{2,1,0:T(8,128)(2,1)} %reduce-scatter.7.cloned.1.call-done), channel_id=1, source_target_pairs={{0,8},{8,16},{16,24},{1,9},{9,17},{17,25},{2,10},{10,18},{18,26},{... | collective-permute-start | bytes 786440 | tf_op jit(solution)/shard_map/ppermute | solution.py:10
  214.5 164.9 %reduce-scatter.11.cloned.1.call-start = ((), (), s32[]{:S(2)}) async-start(), calls=%async_computation.7 | async-start | bytes 2359296 | tf_op jit(solution)/shard_map/reduce_scatter | solution.py:27
  284.7 4.7 %collective-permute-start.2 = (bf16[8,64,256]{2,1,0:T(8,128)(2,1)}, bf16[8,64,256]{2,1,0:T(8,128)(2,1)S(1)}, u32[]{:S(2)}, u32[]{:S(2)}) collective-permute-start(bf16[8,64,256]{2,1,0:T(8,128)(2,1)} %reduce-scatter.9.cloned.1.call-done), channel_id=1, source_target_pairs={{0,8},{8,16},{16,24},{1,9},{9,17},{17,25},{2,10},{10,18},{18,26},{... | collective-permute-start | bytes 786440 | tf_op jit(solution)/shard_map/ppermute | solution.py:10
  306.6 72.8 %copy-start.4 = (bf16[8,64,256]{2,1,0:T(8,128)(2,1)S(1)}, bf16[8,64,256]{2,1,0:T(8,128)(2,1)}, u32[]{:S(2)}) copy-start(bf16[8,64,256]{2,1,0:T(8,128)(2,1)} %reduce-scatter.5.cloned.1.call-done) | copy-start | bytes 786436
  306.6 72.8 %copy-start.5 = (bf16[8,64,256]{2,1,0:T(8,128)(2,1)S(1)}, bf16[8,64,256]{2,1,0:T(8,128)(2,1)}, u32[]{:S(2)}) copy-start(bf16[8,64,256]{2,1,0:T(8,128)(2,1)} %reduce-scatter.7.cloned.1.call-done) | copy-start | bytes 786436
  306.6 72.8 %copy-start.6 = (bf16[8,64,256]{2,1,0:T(8,128)(2,1)S(1)}, bf16[8,64,256]{2,1,0:T(8,128)(2,1)}, u32[]{:S(2)}) copy-start(bf16[8,64,256]{2,1,0:T(8,128)(2,1)} %reduce-scatter.9.cloned.1.call-done) | copy-start | bytes 786436
Sparse Core Ops, SparseCore 0:
  29.6 67.3 reduce-scatter.4
  120.8 69.9 reduce-scatter.6
  214.6 70.0 reduce-scatter.8
  309.3 70.0 reduce-scatter.10
where the time goes:
time: 391 us; the launch traced here: 388 us
  waiting for transfers between devices  288 us (74%)
  local copies, waits for them, and re-layouts  56.5 us (14%)
  matrix products  22.5 us (6%)
  between operations  14 us (4%)
  starting transfers between devices  4.66 us (1%)
    reduce_scatter x4, waiting for transfers between devices, advance(): lax.psum_scatter(partial_value.astype(jnp.bfloat16), 'col', scatter_dimen...  278 us
    dot_general x8, local copies, waits for them, and re-layouts, solve_part(): jnp.dot(onehot, flat_tiles, preferred_element_type=jnp.float32)  35.7 us
    unnamed x18, local copies, waits for them, and re-layouts  19.5 us
    dot_general x4, matrix products, solve_part(): jnp.dot(onehot, flat_tiles, preferred_element_type=jnp.float32)  15 us
    ppermute x3, waiting for transfers between devices, shifted(): return lax.ppermute(value, axis, pairs)  9.53 us
  transfers between devices with their start and end apart: 7, of which 7 were waited for; matrix products, arithmetic and copies ran while one was open for 0% of the time, Pallas kernels for 0%

commit v1 on v0

v1 whole, which is shorter than its diff:
```python
import functools

import jax
import jax.numpy as jnp
from jax import lax
from jax.experimental import pallas as pl
from jax.experimental.pallas import tpu as pltpu
from jax.sharding import PartitionSpec as P

MESH = pl.DeviceIdType.MESH


def low_size(n_col):
    low = 1
    while (2 * low) ** 2 <= n_col:
        low *= 2
    return low


def kernel(
    dims, idx_ref, rhs_ref, diag_ref, off_ref, sol_ref, hand_ref,
    a_ref, x_ref, inc, send1, recv1, send2, recv2, acc, passed,
    s1_sem, r1_sem, s2_sem, r2_sem, sp_sem, rp_sem,
):
    n_sec, n_hi, n_lo, chunks, nc = dims
    blocks, width, _ = rhs_ref.shape
    noff = off_ref.shape[1]
    rows = idx_ref.shape[1]
    sec = lax.axis_index("sec")
    col = lax.axis_index("col")
    hi, lo = col // n_lo, col % n_lo
    size = blocks * width

    def lo_peer(o):
        return {"sec": sec, "col": hi * n_lo + lax.rem(lo + o, n_lo)}

    def hi_peer(o):
        return {"sec": sec, "col": lax.rem(hi + o, n_hi) * n_lo + lo}

    def next_sec():
        return {"sec": lax.rem(sec + 1, n_sec), "col": col}

    barrier = pltpu.get_barrier_semaphore()
    for o in range(1, n_lo):
        pl.semaphore_signal(barrier, inc=1, device_id=lo_peer(o), device_id_type=MESH)
    for o in range(1, n_hi):
        pl.semaphore_signal(barrier, inc=1, device_id=hi_peer(o), device_id_type=MESH)

    for by in (1, n_sec - 1):
        pl.semaphore_signal(
            barrier, inc=1, device_id={"sec": lax.rem(sec + by, n_sec), "col": col},
            device_id_type=MESH,
        )

    @pl.when(sec == 0)
    def _():
        inc[...] = jnp.zeros_like(inc)

    def build(i, carry):
        for pair in range(blocks // 2):
            parts = []
            for k in (2 * pair, 2 * pair + 1):
                p = idx_ref[k, i]
                tile = off_ref[k, jnp.minimum(p, noff - 1)]
                parts.append(jnp.where(p < noff, tile, jnp.zeros_like(tile)))
            a_ref[i, :, 2 * pair * width:2 * (pair + 1) * width] = jnp.concatenate(parts, axis=1)
        return carry

    lax.fori_loop(0, rows, build, 0)

    pl.semaphore_wait(barrier, n_lo - 1 + n_hi - 1 + 2)

    def copy1(j, o, oh):
        return pltpu.make_async_remote_copy(
            src_ref=send1.at[j, o - 1, oh], dst_ref=recv1.at[j, o - 1, oh],
            send_sem=s1_sem.at[j, o - 1, oh], recv_sem=r1_sem.at[j, o - 1, oh],
            device_id=lo_peer(o), device_id_type=MESH,
        )

    def copy2(j, oh):
        return pltpu.make_async_remote_copy(
            src_ref=send2.at[j, oh - 1], dst_ref=recv2.at[j, oh - 1],
            send_sem=s2_sem.at[j, oh - 1], recv_sem=r2_sem.at[j, oh - 1],
            device_id=hi_peer(oh), device_id_type=MESH,
        )

    def copyp(j):
        return pltpu.make_async_remote_copy(
            src_ref=passed.at[j], dst_ref=inc.at[j],
            send_sem=sp_sem.at[j], recv_sem=rp_sem.at[j],
            device_id=next_sec(), device_id_type=MESH,
        )

    order = list(range(1, n_hi)) + [0]

    def product(j, oh, o):
        dest = lax.rem(hi + oh, n_hi) * n_lo + lax.rem(lo + o, n_lo)
        a = a_ref[pl.ds(dest * blocks, blocks)].reshape(size, size)
        return jnp.dot(a, x_ref[j], preferred_element_type=jnp.float32)

    def first(j):
        @pl.when(sec > 0)
        def _():
            copyp(j).wait_recv()

        cols = slice(j * nc, (j + 1) * nc)
        for k in range(blocks):
            part = slice(k * width, (k + 1) * width)
            residual = (
                rhs_ref[k, :, cols].astype(jnp.float32) - inc[j, part, :].astype(jnp.float32)
            ).astype(jnp.bfloat16)
            solved = jnp.dot(
                diag_ref[k], residual, preferred_element_type=jnp.float32
            ).astype(jnp.bfloat16)
            x_ref[j, part, :] = solved
            sol_ref[k, :, cols] = solved
        for oh in order:
            for o in range(1, n_lo):
                send1[j, o - 1, oh] = product(j, oh, o).astype(jnp.bfloat16)
                copy1(j, o, oh).start()

    def middle(j):
        for oh in order:
            total = product(j, oh, 0)
            for o in range(1, n_lo):
                copy1(j, o, oh).wait_recv()
                total = total + recv1[j, o - 1, oh].astype(jnp.float32)
            if oh == 0:
                acc[j] = total
            else:
                send2[j, oh - 1] = total.astype(jnp.bfloat16)
                copy2(j, oh).start()

    def last(j):
        total = acc[j]
        for oh in range(1, n_hi):
            copy2(j, oh).wait_recv()
            total = total + recv2[j, oh - 1].astype(jnp.float32)
        passed[j] = total.astype(jnp.bfloat16)

        @pl.when(sec < n_sec - 1)
        def _():
            copyp(j).start()

        hand_ref[:, :, j * nc:(j + 1) * nc] = passed[j].reshape(blocks, width, nc)

    first(0)
    middle(0)
    for j in range(chunks):
        if j + 1 < chunks:
            first(j + 1)
        last(j)
        if j + 1 < chunks:
            middle(j + 1)

    for j in range(chunks):
        for o in range(1, n_lo):
            for oh in range(n_hi):
                copy1(j, o, oh).wait_send()
        for oh in range(1, n_hi):
            copy2(j, oh).wait_send()

        @pl.when(sec < n_sec - 1)
        def _():
            copyp(j).wait_send()


def shards(n_sec, n_col, rhs, diag_inv, off_tiles, targets, row_slot):
    blocks, width, columns = rhs.shape
    noff = off_tiles.shape[1]
    rows = row_slot.shape[1]
    n_lo = low_size(n_col)
    n_hi = n_col // n_lo
    nc = 128
    chunks = columns // nc
    size = blocks * width
    hit = (targets[:, None, :, None] == jnp.arange(rows, dtype=jnp.int32)[None, None, None, :]) & (
        row_slot[0][None, None, None, :] == jnp.arange(rows, dtype=jnp.int32)[None, :, None, None]
    )
    place = jnp.arange(noff, dtype=jnp.int32)[None, None, :, None]
    idx = jnp.min(jnp.where(hit, place, noff), axis=(2, 3))

    vmem = pl.BlockSpec(memory_space=pltpu.VMEM)
    out = jax.ShapeDtypeStruct((blocks, width, columns), jnp.bfloat16)
    dma = pltpu.SemaphoreType.DMA
    bf16 = jnp.bfloat16
    return pl.pallas_call(
        functools.partial(kernel, (n_sec, n_hi, n_lo, chunks, nc)),
        out_shape=(out, out),
        in_specs=[pl.BlockSpec(memory_space=pltpu.SMEM), vmem, vmem, vmem],
        out_specs=(vmem, vmem),
        scratch_shapes=[
            pltpu.VMEM((rows, width, size), bf16),
            pltpu.VMEM((chunks, size, nc), bf16),
            pltpu.VMEM((chunks, size, nc), bf16),
            pltpu.VMEM((chunks, n_lo - 1, n_hi, size, nc), bf16),
            pltpu.VMEM((chunks, n_lo - 1, n_hi, size, nc), bf16),
            pltpu.VMEM((chunks, n_hi - 1, size, nc), bf16),
            pltpu.VMEM((chunks, n_hi - 1, size, nc), bf16),
            pltpu.VMEM((chunks, size, nc), jnp.float32),
            pltpu.VMEM((chunks, size, nc), bf16),
            dma((chunks, n_lo - 1, n_hi)),
            dma((chunks, n_lo - 1, n_hi)),
            dma((chunks, n_hi - 1)),
            dma((chunks, n_hi - 1)),
            dma((chunks,)),
            dma((chunks,)),
        ],
        compiler_params=pltpu.CompilerParams(
            collective_id=0, has_side_effects=True, vmem_limit_bytes=40 * 1024 * 1024
        ),
    )(idx, rhs, diag_inv, off_tiles)


def solution(mesh):
    return jax.shard_map(
        functools.partial(shards, mesh.shape["sec"], mesh.shape["col"]),
        mesh=mesh,
        in_specs=(
            P(("sec", "col"), None, None),
            P(("sec", "col"), None, None),
            P(("sec", "col"), None, None, None),
            P(("sec", "col"), None),
            P("sec", None),
        ),
        out_specs=(P(("sec", "col"), None, None), P(("sec", "col"), None, None)),
        check_vma=False,
    )
```

time: 391 us -> 96.2 us (0.25)
  waiting for transfers between devices: 288 us -> 0 us
  Pallas kernels: 0 us -> 79.8 us
  local copies, waits for them, and re-layouts: 56.5 us -> 4.85 us
  matrix products: 22.5 us -> 0 us
  between operations: 14 us -> 0.66 us
  other arithmetic: 2.54 us -> 10.7 us
  starting transfers between devices: 4.66 us -> 0 us
    reduce_scatter x4 -> x0, waiting for transfers between devices: 278 us -> none  [advance(): lax.psum_scatter(partial_value.astype(jnp.bfloat16), 'col', scatter_dimen...]
    pallas_call x0 -> x1, Pallas kernels: none -> 79.8 us  [shards(): pl.pallas_call(functools.partial(kernel, (n_sec, n_hi, n_lo, chunks, nc))...]
    dot_general x8 -> x0, local copies, waits for them, and re-layouts: 35.7 us -> none  [solve_part(): jnp.dot(onehot, flat_tiles, preferred_element_type=jnp.float32)]
    dot_general x12 -> x0, matrix products: 22.5 us -> none  [the longest x4 15 us: solve_part(): jnp.dot(onehot, flat_tiles, preferred_element_type=jnp.float32)]
    unnamed x18 -> x8, local copies, waits for them, and re-layouts: 19.5 us -> 4.85 us
    ppermute x3 -> x0, waiting for transfers between devices: 9.53 us -> none  [shifted(): return lax.ppermute(value, axis, pairs)]
    reduce_min x0 -> x1, other arithmetic: none -> 9.22 us  [shards(): idx = jnp.min(jnp.where(hit, place, noff), axis=(2, 3))]
    ppermute x3 -> x0, starting transfers between devices: 4.5 us -> none  [shifted(): return lax.ppermute(value, axis, pairs)]
  transfers between devices with their start and end apart: 7 -> 0, of which waited for: 7 -> 0; matrix products, arithmetic and copies ran while one was open for 0% -> 0% of each run, Pallas kernels for 0% -> 0%
where the time goes in v1:
time: 96.2 us; the launch traced here: 95.9 us
  Pallas kernels  79.8 us (83%)
  other arithmetic  10.7 us (11%)
  local copies, waits for them, and re-layouts  4.85 us (5%)
    pallas_call x1, Pallas kernels, shards(): pl.pallas_call(functools.partial(kernel, (n_sec, n_hi, n_lo, chunks, nc))...  79.8 us
    reduce_min x1, other arithmetic, shards(): idx = jnp.min(jnp.where(hit, place, noff), axis=(2, 3))  9.22 us
    unnamed x8, local copies, waits for them, and re-layouts  4.85 us

profile of v1, /device:TPU:7, one launch (start us, length us, event | category | flops | bytes accessed | tf_op | source)
XLA Modules:
  0.0 95.9 jit_solution(17186112773725842368)
XLA Ops:
  0.6 0.7 iota_compare_fusion.1
  1.3 0.8 iota_compare_fusion
  2.1 9.2 %select_reduce_fusion.idx_ref = s32[8,64]{1,0:T(8,128)S(1)} fusion(pred[64,64]{1,0:T(8,128)(4,1)S(1)} %iota_compare_fusion.1, pred[8,16,64]{2,1,0:T(8,128)(4,1)S(1)} %iota_compare_fusion), kind=kLoop, calls=%fused_computation | loop fusion | flops 1572352 | bytes 14336 | tf_op jit(solution)/shard_map/reduce_min | solution.py:181
  11.3 0.0 copy-start
  11.3 1.6 %copy-done = bf16[8,16,64,64]{3,2,1,0:T(8,128)(2,1)S(1)} copy-done((bf16[8,16,64,64]{3,2,1,0:T(8,128)(2,1)S(1)}, bf16[8,16,64,64]{3,2,1,0:T(8,128)(2,1)}, u32[]{:S(2)}) %copy-start) | copy-done | bytes 1048600
  12.9 0.0 copy-start.1
  12.9 0.9 copy-done.1
  13.8 0.0 copy-start.2
  13.8 0.9 copy-done.2
  14.7 79.8 %shard_map.68 = (bf16[8,64,256]{2,1,0:T(8,128)(2,1)S(1)}, bf16[8,64,256]{2,1,0:T(8,128)(2,1)S(1)}) custom-call(s32[8,64]{1,0:T(8,128)S(1)} %select_reduce_fusion.idx_ref, bf16[8,64,256]{2,1,0:T(8,128)(2,1)S(1)} %copy-done.1, bf16[8,64,64]{2,1,0:T(8,128)(2,1)S(1)} %copy-done.2, bf16[8,16,64,64]{3,2,1,0:T(8,128)(2,1)S(1)} %copy-done), custom_call_target="tpu_custom_call" | custom-call | tf_op jit(solution)/shard_map/pallas_call | solution.py:187
  94.5 0.7 copy.9
  95.2 0.7 copy.10
Async XLA Ops:
  11.3 1.6 %copy-start = (bf16[8,16,64,64]{3,2,1,0:T(8,128)(2,1)S(1)}, bf16[8,16,64,64]{3,2,1,0:T(8,128)(2,1)}, u32[]{:S(2)}) copy-start(bf16[8,16,64,64]{3,2,1,0:T(8,128)(2,1)} %off_ref.1) | copy-start | bytes 3145732
  12.9 0.9 copy-start.1
  13.8 0.9 copy-start.2

commit v2 on v1

--- a/solution.py
+++ b/solution.py
@@ -18,14 +18,16 @@
 
 
 def kernel(
-    dims, idx_ref, rhs_ref, diag_ref, off_ref, sol_ref, hand_ref,
+    dims, targets_ref, slot_ref, rhs_hbm, diag_hbm, off_hbm, sol_ref, hand_ref,
+    rhs_ref, diag_ref, off_ref, pack_ref, idx_vec, idx_ref, in_sem,
     a_ref, x_ref, inc, send1, recv1, send2, recv2, acc, passed,
     s1_sem, r1_sem, s2_sem, r2_sem, sp_sem, rp_sem,
 ):
     n_sec, n_hi, n_lo, chunks, nc = dims
     blocks, width, _ = rhs_ref.shape
     noff = off_ref.shape[1]
-    rows = idx_ref.shape[1]
+    rows = slot_ref.shape[1]
+    lanes = idx_vec.shape[1]
     sec = lax.axis_index("sec")
     col = lax.axis_index("col")
     hi, lo = col // n_lo, col % n_lo
@@ -39,6 +41,13 @@
 
     def next_sec():
         return {"sec": lax.rem(sec + 1, n_sec), "col": col}
+
+    load_off = pltpu.make_async_copy(off_hbm, off_ref, in_sem.at[0])
+    load_rhs = pltpu.make_async_copy(rhs_hbm, rhs_ref, in_sem.at[1])
+    load_diag = pltpu.make_async_copy(diag_hbm, diag_ref, in_sem.at[2])
+    load_off.start()
+    load_rhs.start()
+    load_diag.start()
 
     barrier = pltpu.get_barrier_semaphore()
     for o in range(1, n_lo):
@@ -56,18 +65,40 @@
     def _():
         inc[...] = jnp.zeros_like(inc)
 
-    def build(i, carry):
-        for pair in range(blocks // 2):
-            parts = []
-            for k in (2 * pair, 2 * pair + 1):
-                p = idx_ref[k, i]
-                tile = off_ref[k, jnp.minimum(p, noff - 1)]
-                parts.append(jnp.where(p < noff, tile, jnp.zeros_like(tile)))
-            a_ref[i, :, 2 * pair * width:2 * (pair + 1) * width] = jnp.concatenate(parts, axis=1)
+    slot_of_lane = lax.broadcasted_iota(jnp.int32, (1, lanes), 1)
+    for k in range(blocks):
+        found = jnp.full((1, lanes), noff, jnp.int32)
+        for p in range(noff):
+            dest = slot_ref[0, targets_ref[k, p]]
+            found = jnp.where(slot_of_lane == dest, p, found)
+        idx_vec[k:k + 1, :] = found
+    to_scalar = pltpu.make_async_copy(idx_vec, idx_ref, in_sem.at[3])
+    to_scalar.start()
+
+    pairs = blocks // 2
+    load_off.wait()
+    for q in range(pairs):
+        pack_ref[q, noff] = jnp.zeros((width, 2 * width), jnp.bfloat16)
+
+    def pack(p, carry):
+        for q in range(pairs):
+            pack_ref[q, p] = jnp.concatenate([off_ref[2 * q, p], off_ref[2 * q + 1, p]], axis=1)
         return carry
 
-    lax.fori_loop(0, rows, build, 0)
-
+    lax.fori_loop(0, noff, pack, 0)
+    to_scalar.wait()
+    left = lax.broadcasted_iota(jnp.int32, (width, 2 * width), 1) < width
+
+    def build(dest):
+        for r in range(blocks):
+            i = dest * blocks + r
+            for q in range(pairs):
+                a_ref[i, :, 2 * q * width:2 * (q + 1) * width] = jnp.where(
+                    left, pack_ref[q, idx_ref[2 * q, i]], pack_ref[q, idx_ref[2 * q + 1, i]]
+                )
+
+    load_rhs.wait()
+    load_diag.wait()
     pl.semaphore_wait(barrier, n_lo - 1 + n_hi - 1 + 2)
 
     def copy1(j, o, oh):
@@ -95,6 +126,8 @@
 
     def product(j, oh, o):
         dest = lax.rem(hi + oh, n_hi) * n_lo + lax.rem(lo + o, n_lo)
+        if j == 0:
+            build(dest)
         a = a_ref[pl.ds(dest * blocks, blocks)].reshape(size, size)
         return jnp.dot(a, x_ref[j], preferred_element_type=jnp.float32)
 
@@ -174,22 +207,27 @@
     nc = 128
     chunks = columns // nc
     size = blocks * width
-    hit = (targets[:, None, :, None] == jnp.arange(rows, dtype=jnp.int32)[None, None, None, :]) & (
-        row_slot[0][None, None, None, :] == jnp.arange(rows, dtype=jnp.int32)[None, :, None, None]
-    )
-    place = jnp.arange(noff, dtype=jnp.int32)[None, None, :, None]
-    idx = jnp.min(jnp.where(hit, place, noff), axis=(2, 3))
+    lanes = -(-rows // 128) * 128
 
     vmem = pl.BlockSpec(memory_space=pltpu.VMEM)
+    smem = pl.BlockSpec(memory_space=pltpu.SMEM)
+    hbm = pl.BlockSpec(memory_space=pl.ANY)
     out = jax.ShapeDtypeStruct((blocks, width, columns), jnp.bfloat16)
     dma = pltpu.SemaphoreType.DMA
     bf16 = jnp.bfloat16
     return pl.pallas_call(
         functools.partial(kernel, (n_sec, n_hi, n_lo, chunks, nc)),
         out_shape=(out, out),
-        in_specs=[pl.BlockSpec(memory_space=pltpu.SMEM), vmem, vmem, vmem],
+        in_specs=[smem, smem, hbm, hbm, hbm],
         out_specs=(vmem, vmem),
         scratch_shapes=[
+            pltpu.VMEM((blocks, width, columns), bf16),
+            pltpu.VMEM((blocks, width, width), bf16),
+            pltpu.VMEM((blocks, noff, width, width), bf16),
+            pltpu.VMEM((blocks // 2, noff + 1, width, 2 * width), bf16),
+            pltpu.VMEM((blocks, lanes), jnp.int32),
+            pltpu.SMEM((blocks, lanes), jnp.int32),
+            dma((4,)),
             pltpu.VMEM((rows, width, size), bf16),
             pltpu.VMEM((chunks, size, nc), bf16),
             pltpu.VMEM((chunks, size, nc), bf16),
@@ -207,9 +245,9 @@
             dma((chunks,)),
         ],
         compiler_params=pltpu.CompilerParams(
-            collective_id=0, has_side_effects=True, vmem_limit_bytes=40 * 1024 * 1024
+            collective_id=0, has_side_effects=True, vmem_limit_bytes=60 * 1024 * 1024
         ),
-    )(idx, rhs, diag_inv, off_tiles)
+    )(targets, row_slot, rhs, diag_inv, off_tiles)
 
 
 def solution(mesh):

time: 96.2 us -> 81.9 us (0.85)
  other arithmetic: 10.7 us -> 0 us
  Pallas kernels: 79.8 us -> 77.6 us
  local copies, waits for them, and re-layouts: 4.85 us -> 3.34 us
    reduce_min x1 -> x0, other arithmetic: 9.22 us -> none  [shards(): idx = jnp.min(jnp.where(hit, place, noff), axis=(2, 3))]
    pallas_call x1, Pallas kernels: 79.8 us -> 77.6 us  [shards(): pl.pallas_call(functools.partial(kernel, (n_sec, n_hi, n_lo, chunks, nc))...]
    unnamed x8 -> x2, local copies, waits for them, and re-layouts: 4.85 us -> 3.34 us
    eq x2 -> x0, other arithmetic: 1.43 us -> none  [the longest x1 0.77 us: shards(): targets[:, None, :, None]]
where the time goes in v2:
time: 81.9 us; the launch traced here: 81.6 us
  Pallas kernels  77.6 us (95%)
  local copies, waits for them, and re-layouts  3.34 us (4%)
    pallas_call x1, Pallas kernels, shards(): pl.pallas_call(functools.partial(kernel, (n_sec, n_hi, n_lo, chunks, nc))...  77.6 us
    unnamed x2, local copies, waits for them, and re-layouts  3.34 us

profile of v2, /device:TPU:7, one launch (start us, length us, event | category | flops | bytes accessed | tf_op | source)
XLA Modules:
  0.0 81.6 jit_solution(10910865393616613323)
XLA Ops:
  0.6 77.6 %shard_map.68 = (bf16[8,64,256]{2,1,0:T(8,128)(2,1)}, bf16[8,64,256]{2,1,0:T(8,128)(2,1)}) custom-call(s32[8,16]{1,0:T(8,128)} %targets_ref.1, s32[1,64]{1,0:T(1,128)} %slot_ref.1, bf16[8,64,256]{2,1,0:T(8,128)(2,1)} %rhs_hbm.1, bf16[8,64,64]{2,1,0:T(8,128)(2,1)} %diag_hbm.1, bf16[8,16,64,64]{3,2,1,0:T(8,128)(2,1)} %off_hbm.1), custom_call_target="tpu_custom_call" | custom-call | tf_op jit(solution)/shard_map/pallas_call | solution.py:218
  78.3 1.7 %copy.9 = bf16[8,64,256]{2,1,0:T(8,128)(2,1)} copy(bf16[8,64,256]{2,1,0:T(8,128)(2,1)} %get-tuple-element.4) | data formatting | bytes 524288
  79.9 1.7 %copy.10 = bf16[8,64,256]{2,1,0:T(8,128)(2,1)} copy(bf16[8,64,256]{2,1,0:T(8,128)(2,1)} %get-tuple-element.5) | data formatting | bytes 524288

commit v3 on v2

v3 whole, which is shorter than its diff:
```python
import functools

import jax
import jax.numpy as jnp
from jax import lax
from jax.experimental import pallas as pl
from jax.experimental.pallas import tpu as pltpu
from jax.sharding import PartitionSpec as P

MESH = pl.DeviceIdType.MESH
OWN, MIRROR, OTHER = 0, 1, 2


def low_size(n_col):
    low = 1
    while (2 * low) ** 2 <= n_col:
        low *= 2
    return low


def kernel(
    dims, targets_ref, slot_ref, rhs_hbm, diag_hbm, off_hbm, sol_ref, hand_ref,
    rin, diag_ref, off_ref, pack_own, pack_mirror, idx_vec, idx_ref,
    a_ref, x_ref, inc, send1, recv1, send2, recv2, acc, passed, ret,
    in_sem, fs_sem, fr_sem, s1_sem, r1_sem, s2_sem, r2_sem, sp_sem, rp_sem, sr_sem, rr_sem,
):
    n_sec, n_hi, n_lo = dims
    half = n_sec // 2
    blocks, width = off_hbm.shape[0], off_hbm.shape[2]
    noff = off_hbm.shape[1]
    rows = slot_ref.shape[1]
    lanes = idx_vec.shape[2]
    nc = rin.shape[3]
    size = blocks * width
    pairs = blocks // 2
    sec = lax.axis_index("sec")
    col = lax.axis_index("col")
    plane, place = sec // half, sec % half
    hi, lo = col // n_lo, col % n_lo
    mirror = {"sec": lax.rem(sec + half, n_sec), "col": col}

    def columns_of(which):
        return pl.ds(pl.multiple_of(which * nc, nc), nc)

    loads = [
        pltpu.make_async_copy(off_hbm, off_ref, in_sem.at[0]),
        pltpu.make_async_copy(diag_hbm, diag_ref.at[OWN], in_sem.at[1]),
        pltpu.make_async_copy(rhs_hbm.at[:, :, columns_of(plane)], rin.at[OWN], in_sem.at[2]),
        pltpu.make_async_copy(rhs_hbm.at[:, :, columns_of(1 - plane)], rin.at[OTHER], in_sem.at[3]),
    ]
    for load in loads:
        load.start()

    def lo_peer(o):
        return {"sec": sec, "col": hi * n_lo + lax.rem(lo + o, n_lo)}

    def hi_peer(o):
        return {"sec": sec, "col": lax.rem(hi + o, n_hi) * n_lo + lo}

    barrier = pltpu.get_barrier_semaphore()
    for o in range(1, n_lo):
        pl.semaphore_signal(barrier, inc=1, device_id=lo_peer(o), device_id_type=MESH)
    for o in range(1, n_hi):
        pl.semaphore_signal(barrier, inc=1, device_id=hi_peer(o), device_id_type=MESH)
    for o in range(1, n_sec):
        pl.semaphore_signal(
            barrier, inc=1, device_id={"sec": lax.rem(sec + o, n_sec), "col": col},
            device_id_type=MESH,
        )

    slot_of_lane = lax.broadcasted_iota(jnp.int32, (1, lanes), 1)
    for k in range(blocks):
        found = jnp.full((1, lanes), noff, jnp.int32)
        for p in range(noff):
            dest = slot_ref[0, targets_ref[k, p]]
            found = jnp.where(slot_of_lane == dest, p, found)
        idx_vec[OWN, k:k + 1, :] = found
    to_scalar = pltpu.make_async_copy(idx_vec.at[OWN], idx_ref.at[OWN], in_sem.at[4])
    to_scalar.start()

    packs = (pack_own, pack_mirror)
    for pack_ref in packs:
        for q in range(pairs):
            pack_ref[q, noff] = jnp.zeros((width, 2 * width), jnp.bfloat16)
    for load in loads:
        load.wait()

    def pack(p, carry):
        for q in range(pairs):
            pack_own[q, p] = jnp.concatenate([off_ref[2 * q, p], off_ref[2 * q + 1, p]], axis=1)
        return carry

    lax.fori_loop(0, noff, pack, 0)
    to_scalar.wait()
    pl.semaphore_wait(barrier, n_lo - 1 + n_hi - 1 + n_sec - 1)

    def factor_copies():
        ends = [
            (idx_vec.at[OWN], idx_vec.at[MIRROR]),
            (diag_ref.at[OWN], diag_ref.at[MIRROR]),
            (rin.at[OTHER], rin.at[MIRROR]),
        ] + [
            (pack_own.at[q, pl.ds(0, noff)], pack_mirror.at[q, pl.ds(0, noff)])
            for q in range(pairs)
        ]
        return [
            pltpu.make_async_remote_copy(
                src_ref=src, dst_ref=dst, send_sem=fs_sem.at[n], recv_sem=fr_sem.at[n],
                device_id=mirror, device_id_type=MESH,
            )
            for n, (src, dst) in enumerate(ends)
        ]

    @pl.when(sec != 0)
    def _():
        for copy in factor_copies():
            copy.start()

    def mirror_factor():
        for copy in factor_copies():
            copy.wait_recv()
        to_scalar = pltpu.make_async_copy(idx_vec.at[MIRROR], idx_ref.at[MIRROR], in_sem.at[5])
        to_scalar.start()
        to_scalar.wait()

    def source(role):
        return lax.rem(role + plane, 2)

    left = lax.broadcasted_iota(jnp.int32, (width, 2 * width), 1) < width

    def build_row(role, src, i):
        pack_ref = packs[src]
        for q in range(pairs):
            a_ref[role, i, :, 2 * q * width:2 * (q + 1) * width] = jnp.where(
                left,
                pack_ref[q, idx_ref[src, 2 * q, i]],
                pack_ref[q, idx_ref[src, 2 * q + 1, i]],
            )

    def build_all(role):
        for src in (OWN, MIRROR):
            @pl.when(source(role) == src)
            def _():
                def step(i, carry):
                    build_row(role, src, i)
                    return carry

                lax.fori_loop(0, rows, step, 0)

    def copy1(j, o, oh):
        return pltpu.make_async_remote_copy(
            src_ref=send1.at[j, o - 1, oh], dst_ref=recv1.at[j, o - 1, oh],
            send_sem=s1_sem.at[j, o - 1, oh], recv_sem=r1_sem.at[j, o - 1, oh],
            device_id=lo_peer(o), device_id_type=MESH,
        )

    def copy2(j, oh):
        return pltpu.make_async_remote_copy(
            src_ref=send2.at[j, oh - 1], dst_ref=recv2.at[j, oh - 1],
            send_sem=s2_sem.at[j, oh - 1], recv_sem=r2_sem.at[j, oh - 1],
            device_id=hi_peer(oh), device_id_type=MESH,
        )

    def copyp(j, to_sec, slot):
        return pltpu.make_async_remote_copy(
            src_ref=passed.at[j], dst_ref=inc.at[slot],
            send_sem=sp_sem.at[j], recv_sem=rp_sem.at[slot],
            device_id={"sec": to_sec, "col": col}, device_id_type=MESH,
        )

    def pass_on(j):
        if j == 0:
            return copyp(0, half + 1, 0)
        more = place + 1 < half
        to_sec = plane * half + jnp.where(more, place + 1, 0)
        if j == 1:
            return copyp(1, to_sec, jnp.where(more, 0, 1))
        return copyp(2, to_sec, 1)

    def give_back(which, j):
        return pltpu.make_async_remote_copy(
            src_ref=(x_ref, passed)[which].at[j], dst_ref=ret.at[which],
            send_sem=sr_sem.at[which], recv_sem=rr_sem.at[which],
            device_id=mirror, device_id_type=MESH,
        )

    order = list(range(1, n_hi)) + [0]

    def product(j, oh, o):
        role = max(j - 1, 0)
        dest = lax.rem(hi + oh, n_hi) * n_lo + lax.rem(lo + o, n_lo)
        if j == 0:
            for r in range(blocks):
                build_row(0, OWN, dest * blocks + r)
        a = a_ref[role, pl.ds(dest * blocks, blocks)].reshape(size, size)
        return jnp.dot(a, x_ref[j], preferred_element_type=jnp.float32)

    def first(j, fresh):
        role = max(j - 1, 0)
        src = source(role)
        which = OTHER if j == 0 else src
        if not fresh:
            copyp(j, sec, role).wait_recv()
        for k in range(blocks):
            part = slice(k * width, (k + 1) * width)
            residual = rin[which, k]
            if not fresh:
                residual = (
                    residual.astype(jnp.float32) - inc[role, part, :].astype(jnp.float32)
                ).astype(jnp.bfloat16)
            x_ref[j, part, :] = jnp.dot(
                diag_ref[src, k], residual, preferred_element_type=jnp.float32
            ).astype(jnp.bfloat16)
        for oh in order:
            for o in range(1, n_lo):
                send1[j, o - 1, oh] = product(j, oh, o).astype(jnp.bfloat16)
                copy1(j, o, oh).start()

    def middle(j):
        for oh in order:
            total = product(j, oh, 0)
            for o in range(1, n_lo):
                copy1(j, o, oh).wait_recv()
                total = total + recv1[j, o - 1, oh].astype(jnp.float32)
            if oh == 0:
                acc[j] = total
            else:
                send2[j, oh - 1] = total.astype(jnp.bfloat16)
                copy2(j, oh).start()

    def last(j):
        total = acc[j]
        for oh in range(1, n_hi):
            copy2(j, oh).wait_recv()
            total = total + recv2[j, oh - 1].astype(jnp.float32)
        passed[j] = total.astype(jnp.bfloat16)
        if j < 2:
            pass_on(j).start()
        else:
            @pl.when(place < half - 1)
            def _():
                pass_on(j).start()

        if j > 0:
            @pl.when(source(j - 1) == MIRROR)
            def _():
                give_back(0, j).start()
                give_back(1, j).start()

    def sent(j):
        for oh in range(n_hi):
            for o in range(1, n_lo):
                copy1(j, o, oh).wait_send()
        for oh in range(1, n_hi):
            copy2(j, oh).wait_send()

    @pl.when(sec == 0)
    def _():
        first(0, True)
        middle(0)
        first(1, True)
        last(0)
        middle(1)
        last(1)
        sent(0)
        sent(1)
        pass_on(0).wait_send()
        pass_on(1).wait_send()

    @pl.when(place > 0)
    def _():
        @pl.when(plane == 1)
        def _():
            mirror_factor()

        build_all(0)
        first(1, False)
        middle(1)
        last(1)
        sent(1)
        pass_on(1).wait_send()

    @pl.when(plane == 0)
    def _():
        mirror_factor()

    build_all(1)
    first(2, False)
    middle(2)
    last(2)
    own = 1 + plane
    sol_ref[:, :, columns_of(plane)] = x_ref[own].reshape(blocks, width, nc)
    hand_ref[:, :, columns_of(plane)] = passed[own].reshape(blocks, width, nc)

    @pl.when(sec == 0)
    def _():
        sol_ref[:, :, nc:2 * nc] = x_ref[0].reshape(blocks, width, nc)
        hand_ref[:, :, nc:2 * nc] = passed[0].reshape(blocks, width, nc)

    @pl.when(sec != 0)
    def _():
        give_back(0, 1).wait_recv()
        sol_ref[:, :, columns_of(1 - plane)] = ret[0].reshape(blocks, width, nc)
        give_back(1, 1).wait_recv()
        hand_ref[:, :, columns_of(1 - plane)] = ret[1].reshape(blocks, width, nc)
        for copy in factor_copies():
            copy.wait_send()

    sent(2)

    @pl.when(place < half - 1)
    def _():
        pass_on(2).wait_send()

    @pl.when(sec != half)
    def _():
        give_back(0, 1).wait_send()
        give_back(1, 1).wait_send()


def shards(n_sec, n_col, rhs, diag_inv, off_tiles, targets, row_slot):
    blocks, width, columns = rhs.shape
    noff = off_tiles.shape[1]
    rows = row_slot.shape[1]
    n_lo = low_size(n_col)
    n_hi = n_col // n_lo
    nc = columns // 2
    size = blocks * width
    pairs = blocks // 2
    lanes = -(-rows // 128) * 128

    vmem = pl.BlockSpec(memory_space=pltpu.VMEM)
    smem = pl.BlockSpec(memory_space=pltpu.SMEM)
    hbm = pl.BlockSpec(memory_space=pl.ANY)
    out = jax.ShapeDtypeStruct((blocks, width, columns), jnp.bfloat16)
    dma = pltpu.SemaphoreType.DMA
    bf16 = jnp.bfloat16
    return pl.pallas_call(
        functools.partial(kernel, (n_sec, n_hi, n_lo)),
        out_shape=(out, out),
        in_specs=[smem, smem, hbm, hbm, hbm],
        out_specs=(vmem, vmem),
        scratch_shapes=[
            pltpu.VMEM((3, blocks, width, nc), bf16),
            pltpu.VMEM((2, blocks, width, width), bf16),
            pltpu.VMEM((blocks, noff, width, width), bf16),
            pltpu.VMEM((pairs, noff + 1, width, 2 * width), bf16),
            pltpu.VMEM((pairs, noff + 1, width, 2 * width), bf16),
            pltpu.VMEM((2, blocks, lanes), jnp.int32),
            pltpu.SMEM((2, blocks, lanes), jnp.int32),
            pltpu.VMEM((2, rows, width, size), bf16),
            pltpu.VMEM((3, size, nc), bf16),
            pltpu.VMEM((2, size, nc), bf16),
            pltpu.VMEM((3, n_lo - 1, n_hi, size, nc), bf16),
            pltpu.VMEM((3, n_lo - 1, n_hi, size, nc), bf16),
            pltpu.VMEM((3, n_hi - 1, size, nc), bf16),
            pltpu.VMEM((3, n_hi - 1, size, nc), bf16),
            pltpu.VMEM((3, size, nc), jnp.float32),
            pltpu.VMEM((3, size, nc), bf16),
            pltpu.VMEM((2, size, nc), bf16),
            dma((6,)),
            dma((3 + pairs,)),
            dma((3 + pairs,)),
            dma((3, n_lo - 1, n_hi)),
            dma((3, n_lo - 1, n_hi)),
            dma((3, n_hi - 1)),
            dma((3, n_hi - 1)),
            dma((3,)),
            dma((2,)),
            dma((2,)),
            dma((2,)),
        ],
        compiler_params=pltpu.CompilerParams(
            collective_id=0, has_side_effects=True, vmem_limit_bytes=60 * 1024 * 1024
        ),
    )(targets, row_slot, rhs, diag_inv, off_tiles)


def solution(mesh):
    return jax.shard_map(
        functools.partial(shards, mesh.shape["sec"], mesh.shape["col"]),
        mesh=mesh,
        in_specs=(
            P(("sec", "col"), None, None),
            P(("sec", "col"), None, None),
            P(("sec", "col"), None, None, None),
            P(("sec", "col"), None),
            P("sec", None),
        ),
        out_specs=(P(("sec", "col"), None, None), P(("sec", "col"), None, None)),
        check_vma=False,
    )
```

time: 81.9 us -> 78.3 us (0.956); the launches traced: 81.6 us -> 77 us
  Pallas kernels: 77.6 us -> 73 us
    pallas_call x1, Pallas kernels: 77.6 us -> 73 us  [shards(): pl.pallas_call(functools.partial(kernel, (n_sec, n_hi, n_lo)), out_shape=...]
where the time goes in v3:
time: 78.3 us; the launch traced here: 77 us
  Pallas kernels  73 us (93%)
  local copies, waits for them, and re-layouts  3.34 us (4%)
    pallas_call x1, Pallas kernels, shards(): pl.pallas_call(functools.partial(kernel, (n_sec, n_hi, n_lo)), out_shape=...  73 us
    unnamed x2, local copies, waits for them, and re-layouts  3.34 us

profile of v3, /device:TPU:7, one launch (start us, length us, event | category | flops | bytes accessed | tf_op | source)
XLA Modules:
  0.0 77.0 jit_solution(17544289344612431874)
XLA Ops:
  0.6 73.0 %shard_map.68 = (bf16[8,64,256]{2,1,0:T(8,128)(2,1)}, bf16[8,64,256]{2,1,0:T(8,128)(2,1)}) custom-call(s32[8,16]{1,0:T(8,128)} %targets_ref.1, s32[1,64]{1,0:T(1,128)} %slot_ref.1, bf16[8,64,256]{2,1,0:T(8,128)(2,1)} %rhs_hbm.1, bf16[8,64,64]{2,1,0:T(8,128)(2,1)} %diag_hbm.1, bf16[8,16,64,64]{3,2,1,0:T(8,128)(2,1)} %off_hbm.1), custom_call_target="tpu_custom_call" | custom-call | tf_op jit(solution)/shard_map/pallas_call | solution.py:338
  73.6 1.7 %copy.9 = bf16[8,64,256]{2,1,0:T(8,128)(2,1)} copy(bf16[8,64,256]{2,1,0:T(8,128)(2,1)} %get-tuple-element.4) | data formatting | bytes 524288
  75.3 1.7 %copy.10 = bf16[8,64,256]{2,1,0:T(8,128)(2,1)} copy(bf16[8,64,256]{2,1,0:T(8,128)(2,1)} %get-tuple-element.5) | data formatting | bytes 524288

commit v4 on v3

--- a/solution.py
+++ b/solution.py
@@ -54,8 +54,16 @@
     def lo_peer(o):
         return {"sec": sec, "col": hi * n_lo + lax.rem(lo + o, n_lo)}
 
+    def hi_flip(o):
+        value, bit = hi, 1
+        while bit < n_hi:
+            if o & bit:
+                value = value + bit - 2 * bit * ((value // bit) % 2)
+            bit *= 2
+        return value
+
     def hi_peer(o):
-        return {"sec": sec, "col": lax.rem(hi + o, n_hi) * n_lo + lo}
+        return {"sec": sec, "col": hi_flip(o) * n_lo + lo}
 
     barrier = pltpu.get_barrier_semaphore()
     for o in range(1, n_lo):
@@ -184,11 +192,11 @@
             device_id=mirror, device_id_type=MESH,
         )
 
-    order = list(range(1, n_hi)) + [0]
+    order = list(range(n_hi - 1, -1, -1))
 
     def product(j, oh, o):
         role = max(j - 1, 0)
-        dest = lax.rem(hi + oh, n_hi) * n_lo + lax.rem(lo + o, n_lo)
+        dest = hi_flip(oh) * n_lo + lax.rem(lo + o, n_lo)
         if j == 0:
             for r in range(blocks):
                 build_row(0, OWN, dest * blocks + r)

time: 78.3 us -> 75.5 us (0.964)
  Pallas kernels: 73 us -> 71 us
    pallas_call x1, Pallas kernels: 73 us -> 71 us  [shards(): pl.pallas_call(functools.partial(kernel, (n_sec, n_hi, n_lo)), out_shape=...]
where the time goes in v4:
time: 75.5 us; the launch traced here: 74.9 us
  Pallas kernels  71 us (94%)
  local copies, waits for them, and re-layouts  3.34 us (4%)
    pallas_call x1, Pallas kernels, shards(): pl.pallas_call(functools.partial(kernel, (n_sec, n_hi, n_lo)), out_shape=...  71 us
    unnamed x2, local copies, waits for them, and re-layouts  3.34 us

profile of v4, /device:TPU:7, one launch (start us, length us, event | category | flops | bytes accessed | tf_op | source)
XLA Modules:
  0.0 74.9 jit_solution(1940328871548487029)
XLA Ops:
  0.6 71.0 %shard_map.68 = (bf16[8,64,256]{2,1,0:T(8,128)(2,1)}, bf16[8,64,256]{2,1,0:T(8,128)(2,1)}) custom-call(s32[8,16]{1,0:T(8,128)} %targets_ref.1, s32[1,64]{1,0:T(1,128)} %slot_ref.1, bf16[8,64,256]{2,1,0:T(8,128)(2,1)} %rhs_hbm.1, bf16[8,64,64]{2,1,0:T(8,128)(2,1)} %diag_hbm.1, bf16[8,16,64,64]{3,2,1,0:T(8,128)(2,1)} %off_hbm.1), custom_call_target="tpu_custom_call" | custom-call | tf_op jit(solution)/shard_map/pallas_call | solution.py:346
  71.6 1.7 %copy.9 = bf16[8,64,256]{2,1,0:T(8,128)(2,1)} copy(bf16[8,64,256]{2,1,0:T(8,128)(2,1)} %get-tuple-element.4) | data formatting | bytes 524288
  73.3 1.7 %copy.10 = bf16[8,64,256]{2,1,0:T(8,128)(2,1)} copy(bf16[8,64,256]{2,1,0:T(8,128)(2,1)} %get-tuple-element.5) | data formatting | bytes 524288
